TPU v7x, 32 devices: a whole 2x2x4 slice. The times are simulated.
32 devices in a mesh: row: 4 (over y, x), col: 8 (over z, core).
Axes of the slice: x: 2, y: 2, z: 4, core: 2. Of those that a mesh axis runs over, the one named last changes fastest.
Arguments:
- depth: float32 [1024, 4096], P('row', 'col'), may hold values from 0.5 to 3
- bed: float32 [1024, 4096], P('row', 'col'), may hold values from -1 to 1
- mass: float32 [1024, 4096], P('row', 'col'), may hold values from 0.2 to 2
- conduct: float32 [1024, 4096], P('row', 'col'), may hold values from 0.02 to 0.2
- settle: float32 [1024, 4096], P('row', 'col'), may hold values from 0.02 to 0.5
- wet: int32 [1024, 4096], P('row', 'col'), may hold values 0 or 1
- link_block: int32 [16384], P(('row', 'col')), may hold values from 0 to 1023
- link_owner: int32 [16384, 1], P(('row', 'col')), may hold values from 0 to 31; in each aligned block of 512 rows (0 to 511, 512 to 1023, ...) at most 32 rows name the same one
- link_reach: int32 [16384], P(('row', 'col')), may hold values from 0 to 15
- link_coef: float32 [16384], P(('row', 'col')), may hold values from 0.05 to 0.5
- chan_phase: float32 [512, 128], P(('row', 'col')), may hold values from -0.5 to 2
- chan_conc: float32 [512, 128], P(('row', 'col')), may hold values from 0.1 to 1
- chan_area: float32 [512, 128], P(('row', 'col')), may hold values from 2 to 20
Outputs:
- depth_out: float32 [1024, 4096], P('row', 'col')
- mass_out: float32 [1024, 4096], P('row', 'col')
- phase_out: float32 [512, 128], P(('row', 'col'))
- conc_out: float32 [512, 128], P(('row', 'col'))
Inputs may be any that keep to these rules, and one draw needn't show every extreme that they name: `link_block`: block index within a tile. `link_owner`: among the 512 links of one tile, at most 32 name the same owner.
All inputs are finite; a program needn't handle non-finite values. No bound on the sum of `wet` on one device may be relied on, other than what follows from the above.
Results may differ from a plain program's by a relative error of at most 0.00005.
Values sent between devices are 32-bit elements; how exact they have to be, the bound alone decides.
A program may use at most 64 MiB of HBM per device.

v0:
```python
import jax
import jax.numpy as jnp
from jax import lax
from jax.sharding import PartitionSpec as P


def padded_2(block, sides, width):
    for axis, dim in sides:
        count = lax.axis_size(axis)
        forward = [(i, i + 1) for i in range(count - 1)]
        backward = [(target, source) for source, target in forward]
        low = lax.ppermute(
            lax.slice_in_dim(block, block.shape[dim] - width, None, axis=dim), axis, forward
        )
        high = lax.ppermute(lax.slice_in_dim(block, 0, width, axis=dim), axis, backward)
        block = jnp.concatenate([low, block, high], axis=dim)
    return block


def smooth_reach(values):
    left = jnp.concatenate([values[:, :1], values[:, :-1]], axis=1)
    right = jnp.concatenate([values[:, 1:], values[:, -1:]], axis=1)
    return values + 0.25 * (left - 2.0 * values + right)


def body(
    depth,
    bed,
    mass,
    conduct,
    settle,
    wet,
    link_block,
    link_owner,
    link_reach,
    link_coef,
    chan_phase,
    chan_conc,
    chan_area,
):
    tile_y, tile_x = depth.shape
    opened = wet.astype(jnp.float32)
    surface = depth + bed
    stacked = jnp.stack([surface, mass, conduct, opened])
    padded = padded_2(stacked, (("row", 1), ("col", 2)), 1)
    water_gain = jnp.zeros_like(depth)
    mass_gain = jnp.zeros_like(depth)
    for step_y, step_x in ((1, 0), (-1, 0), (0, 1), (0, -1)):
        beside = padded[:, 1 + step_y : 1 + step_y + tile_y, 1 + step_x : 1 + step_x + tile_x]
        coeff = 0.5 * (conduct + beside[2]) * opened * beside[3]
        water_gain = water_gain + coeff * (beside[0] - surface)
        mass_gain = mass_gain + coeff * (beside[1] - mass)
    depth1 = depth + water_gain
    mass1 = (mass + mass_gain) * jnp.exp(-settle)
    surface1 = depth1 + bed
    blocks = tile_y * tile_x // 128
    surf_blocks = surface1.reshape(blocks, 128)
    mass_blocks = mass1.reshape(blocks, 128)
    open_blocks = opened.reshape(blocks, 128)
    surf_rows = surf_blocks[link_block]
    mass_rows = mass_blocks[link_block]
    weight = link_coef[:, None] * open_blocks[link_block]
    lat_rows = jnp.stack([weight * surf_rows, weight * mass_rows, weight], axis=1)
    n_row = lax.axis_size("row")
    n_col = lax.axis_size("col")
    devices = n_row * n_col
    links_here = link_owner.shape[0]
    slot_cap = max(2, 2 * links_here // devices)
    target = link_owner[:, 0]
    owner_hot = (target[:, None] == jnp.arange(devices, dtype=jnp.int32)[None, :]).astype(jnp.int32)
    ranking = jnp.sum((jnp.cumsum(owner_hot, axis=0) - 1) * owner_hot, axis=1)
    slot_of = target * slot_cap + ranking
    outgoing = jnp.zeros((devices * slot_cap, 3, 128), jnp.float32).at[slot_of].set(lat_rows)
    reach_tags = (
        jnp.full((devices * slot_cap,), -1.0, jnp.float32)
        .at[slot_of]
        .set(link_reach.astype(jnp.float32))
    )
    arrived, arrived_tags = (
        lax.all_to_all(
            outgoing.reshape(devices, slot_cap, 3, 128),
            ("row", "col"),
            split_axis=0,
            concat_axis=0,
            tiled=True,
        ),
        lax.all_to_all(
            reach_tags.reshape(devices, slot_cap),
            ("row", "col"),
            split_axis=0,
            concat_axis=0,
            tiled=True,
        ),
    )
    arrived = arrived.reshape(devices * slot_cap, 384)
    arrived_tags = arrived_tags.reshape(devices * slot_cap)
    reach_dev = chan_phase.shape[0]
    reach_hot = (arrived_tags[None, :] == jnp.arange(reach_dev, dtype=jnp.float32)[:, None]).astype(
        jnp.float32
    )
    totals = jnp.dot(reach_hot, arrived, precision=lax.Precision.HIGHEST)
    inflow = totals[:, :128]
    sediment = totals[:, 128:256]
    wet_sum = totals[:, 256:]
    phase_new = (chan_area * chan_phase + inflow) / (chan_area + wet_sum)
    conc_new = (chan_area * chan_conc + sediment) / (chan_area + wet_sum)
    phase_out = smooth_reach(phase_new)
    conc_out = smooth_reach(conc_new)
    reply = jnp.dot(
        reach_hot.T, jnp.concatenate([phase_out, conc_out], axis=1), precision=lax.Precision.HIGHEST
    )
    answered = lax.all_to_all(
        reply.reshape(devices, slot_cap, 256),
        ("row", "col"),
        split_axis=0,
        concat_axis=0,
        tiled=True,
    )
    own_rows = answered.reshape(devices * slot_cap, 256)[slot_of]
    applied = jnp.concatenate(
        [
            0.5 * weight * (own_rows[:, :128] - surf_rows),
            0.5 * weight * (own_rows[:, 128:] - mass_rows),
        ],
        axis=1,
    )
    block_hot = (jnp.arange(blocks, dtype=jnp.int32)[:, None] == link_block[None, :]).astype(
        jnp.float32
    )
    gained = jnp.dot(block_hot, applied, precision=lax.Precision.HIGHEST)
    depth_out = (depth1.reshape(blocks, 128) + gained[:, :128]).reshape(tile_y, tile_x)
    mass_out = (mass_blocks + gained[:, 128:]).reshape(tile_y, tile_x)
    return (depth_out, mass_out, phase_out, conc_out)


def solution(mesh):
    return jax.shard_map(
        body,
        mesh=mesh,
        in_specs=(
            P("row", "col"),
            P("row", "col"),
            P("row", "col"),
            P("row", "col"),
            P("row", "col"),
            P("row", "col"),
            P(("row", "col")),
            P(("row", "col"), None),
            P(("row", "col")),
            P(("row", "col")),
            P(("row", "col"), None),
            P(("row", "col"), None),
            P(("row", "col"), None),
        ),
        out_specs=(
            P("row", "col"),
            P("row", "col"),
            P(("row", "col"), None),
            P(("row", "col"), None),
        ),
        check_vma=False,
    )
```

profile of v0, /device:TPU:1, one launch (start us, length us, event | category | flops | bytes accessed | tf_op | source)
XLA Modules:
  0.0 211.0 jit_solution(7395269289954060707)
XLA Ops:
  0.7 1.2 fusion.76
  1.9 0.5 copy.53
  2.6 0.8 copy-done.10
  3.4 0.5 copy.52
  4.0 0.4 stack.22
  4.7 2.0 pad_maximum_fusion.1
  6.7 1.4 copy-done.5
  8.1 1.3 collective-permute-start
  9.4 4.6 %collective-permute-start.1 = (f32[4,1,512]{2,0,1:T(4,128)S(1)}, f32[4,1,512]{2,0,1:T(4,128)S(1)}, u32[]{:S(2)}, u32[]{:S(2)}) collective-permute-start(f32[4,1,512]{2,0,1:T(4,128)S(1)} %get-tuple-element.16), channel_id=1, source_target_pairs={{0,8},{8,16},{16,24},{1,9},{9,17},{17,25},{2,10},{10,18},{18,26},{... | collective-permute-start | bytes 24584 | tf_op jit(solution)/shard_map/ppermute | solution.py:12
  14.0 1.2 reduce-window.6
  15.6 2.4 %scatter_custom_fusion = f32[1024]{0:T(1024)S(1)} fusion(s32[512]{0:T(512)S(1)} %bitcast.213, f32[512]{0:T(512)S(1)} %convert_element_type.15, f32[]{:T(128)} %constant.4.clone.1), kind=kCustom, calls=%fused_computation.127 | custom fusion | bytes 4100 | tf_op jit(solution)/shard_map/scatter | solution.py:77
  18.0 0.7 all_to_all.12
  18.7 7.0 %all-to-all-start = ((f32[32,1,32]{2,1,0:T(1,128)}), f32[32,1,32]{2,1,0:T(1,128)S(1)}, u32[]{:S(2)}, u32[]{:S(2)}) async-start(f32[32,1,32]{2,1,0:T(1,128)} %all_to_all.12), calls=%async_computation | async-start | bytes 32768 | tf_op jit(solution)/shard_map/all_to_all | solution.py:87
  25.8 4.3 %constant_dynamic-update-slice_fusion = (f32[4,257,512]{2,1,0:T(8,128)}, f32[4,256,512]{2,1,0:T(8,128)}) fusion(f32[4,256,512]{2,0,1:T(4,128)} %copy-done.5), kind=kLoop, calls=%fused_computation.126 | loop fusion | bytes 6291456
  30.1 2.0 pad_maximum_fusion
  32.1 1.4 copy-done
  33.5 1.1 fusion.74
  34.9 3.5 %collective-permute-start.3 = (f32[4,258,1]{1,0,2:T(4,128)S(1)}, f32[4,258,1]{1,0,2:T(4,128)S(1)}, u32[]{:S(2)}, u32[]{:S(2)}) collective-permute-start(f32[4,258,1]{1,0,2:T(4,128)S(1)} %copy.61), channel_id=1, source_target_pairs={{0,1},{1,2},{2,3},{3,4},{4,5},{5,6},{6,7},{8,9},{9,10},{10,11},{11... | collective-permute-start | bytes 12392 | tf_op jit(solution)/shard_map/ppermute | solution.py:12
  38.5 1.0 gather_fusion
  39.5 2.3 %copy.59 = f32[4,258,512]{2,1,0:T(8,128)S(1)} copy(f32[4,258,512]{2,0,1:T(4,128)} %copy-done) | data formatting | bytes 4227072 | tf_op jit(solution)/shard_map/concatenate | solution.py:16
  41.8 1.3 copy.58
  43.1 2.1 collective-permute-start.2
  45.3 1.5 dynamic-update-slice.1
  46.8 1.1 copy.62
  47.9 15.4 %pad_maximum_fusion.13 = (f32[1,256,512]{2,0,1:T(1,128)}, f32[1,256,512]{2,0,1:T(1,128)}) fusion(f32[4,258,1]{2,0,1:T(4,128)} %copy.62, f32[4,1,512]{2,0,1:T(4,128)S(1)} %collective-permute-done, f32[4,1,512]{2,0,1:T(4,128)S(1)} %collective-permute-done.1, f32[1,256,512]{2,0,1:T(1,128)S(1)} %copy.53, f32[1,256,512]{2,0,1:T(1,128)} %copy-done.3, ...), kind=kLoop, calls=%fused_computation.41 | loop fusion | flops 1572864 | bytes 3166240 | tf_op jit(solution)/shard_map/slice | solution.py:50
  63.4 14.2 %pad_maximum_fusion.3 = (f32[1,256,512]{2,0,1:T(1,128)}, f32[1,256,512]{2,0,1:T(1,128)}) fusion(f32[4,258,1]{2,0,1:T(4,128)S(1)} %copy-done.7, f32[4,1,512]{2,0,1:T(4,128)S(1)} %collective-permute-done, f32[4,1,512]{2,0,1:T(4,128)S(1)} %collective-permute-done.1, f32[1,256,512]{2,0,1:T(1,128)S(1)} %copy.53, f32[1,256,512]{2,0,1:T(1,128)S(1)} %copy-done.4, ...), kind=kLoop, calls=%fused_computation.17 | loop fusion | flops 1572864 | bytes 3166240 | tf_op jit(solution)/shard_map/concatenate | solution.py:16
  77.9 5.3 %fusion.72 = (f32[256,512]{1,0:T(8,128)}, f32[256,512]{1,0:T(8,128)}) fusion(f32[256,512]{1,0:T(8,128)} %param.14, f32[256,512]{1,0:T(8,128)} %param.13, f32[256,512]{1,0:T(8,128)} %copy-done.10, f32[1,256,512]{2,0,1:T(1,128)} %get-tuple-element.9, f32[1,256,512]{2,0,1:T(1,128)} %get-tuple-element.11, f32[256,512]{1,0:T(8,128)} %param.16, ...), kind=kLoop, calls=%fused_computation.132 | loop fusion | flops 4718592 | bytes 11038752 | tf_op jit(solution)/shard_map/add | solution.py:55
  83.3 1.1 reshape.145
  84.4 1.6 gather_fusion.1
  86.0 4.8 %fusion.11 = f32[256,512]{1,0:T(8,128)} fusion(f32[256,512]{1,0:T(8,128)} %param.15, f32[4,258,1]{2,1,0:T(8,128)} %copy-done.6, f32[4,258,512]{2,1,0:T(8,128)S(1)} %copy.59, f32[4,256,512]{2,1,0:T(8,128)} %get-tuple-element.15, f32[4,1,512]{2,1,0:T(1,128)S(1)} %copy.56, f32[4,257,512]{2,1,0:T(8,128)} %dynamic-update-slice.1, f32[256,512]{1,0:T(8,128)} %param.16, ...), kind=kLoop, calls=%fused_computation.30 | loop fusion | flops 4849664 | bytes 9990176 | tf_op jit(solution)/shard_map/mul | solution.py:54
  90.8 1.1 reshape.146
  92.0 1.0 gather_fusion.2
  93.3 1.5 copy.67
  95.1 31.4 %scatter_fusion = f32[1024,3,128]{2,1,0:T(4,128)S(1)} fusion(f32[1024,3,128]{2,1,0:T(4,128)S(1)} %broadcast_in_dim.8, s32[512]{0:T(512)S(1)} %bitcast.214, f32[512,3,128]{2,1,0:T(4,128)} %copy.67), kind=kCustom, calls=%fused_computation.5 | custom fusion | bytes 2361344 | tf_op jit(solution)/shard_map/scatter | solution.py:73
  126.5 1.4 copy.68
  127.9 5.9 %all-to-all-start.1 = ((f32[32,32,3,128]{3,1,2,0:T(8,128)}), f32[32,32,3,128]{3,1,2,0:T(8,128)S(1)}, u32[]{:S(2)}, u32[]{:S(2)}) async-start(f32[32,32,3,128]{3,1,2,0:T(8,128)} %copy.68), calls=%async_computation.1 | async-start | bytes 3145728 | tf_op jit(solution)/shard_map/all_to_all | solution.py:80
  133.8 0.5 broadcast.134
  134.3 0.7 reduce.5
  135.1 37.0 %all-to-all-done.1 = f32[32,32,3,128]{3,1,2,0:T(8,128)S(1)} async-done(((f32[32,32,3,128]{3,1,2,0:T(8,128)}), f32[32,32,3,128]{3,1,2,0:T(8,128)S(1)}, u32[]{:S(2)}, u32[]{:S(2)}) %all-to-all-start.1) | async-done | bytes 1572896 | tf_op jit(solution)/shard_map/all_to_all | solution.py:80
  172.1 1.3 copy.69
  173.4 0.6 fusion.1
  174.4 1.6 fusion.53
  176.1 3.1 %all-to-all-start.2 = ((f32[32,32,256]{2,1,0:T(8,128)}), f32[32,32,256]{2,1,0:T(8,128)S(1)}, u32[]{:S(2)}, u32[]{:S(2)}) async-start(f32[32,32,256]{2,1,0:T(8,128)} %bitcast.26), calls=%async_computation.2 | async-start | bytes 2097152 | tf_op jit(solution)/shard_map/all_to_all | solution.py:112
  179.2 27.0 %all-to-all-done.2 = f32[32,32,256]{2,1,0:T(8,128)S(1)} async-done(((f32[32,32,256]{2,1,0:T(8,128)}), f32[32,32,256]{2,1,0:T(8,128)S(1)}, u32[]{:S(2)}, u32[]{:S(2)}) %all-to-all-start.2) | async-done | bytes 1048608 | tf_op jit(solution)/shard_map/all_to_all | solution.py:112
  206.3 1.6 gather_fusion.3
  208.0 1.1 fusion
  209.2 0.9 reshape.151
  210.1 0.9 reshape.152
  (86 shorter events, 2.8 us)
Async XLA Ops:
  0.6 1.8 copy-start.12
  0.6 1.8 copy-start.13
  1.9 2.0 copy-start.14
  2.5 1.8 copy-start.9
  2.6 0.8 copy-start.10
  4.3 25.7 %copy-start.1 = (f32[1,256,512]{2,0,1:T(1,128)}, f32[1,256,512]{2,0,1:T(1,128)S(1)}, u32[]{:S(2)}) copy-start(f32[1,256,512]{2,0,1:T(1,128)S(1)} %stack.22) | copy-start | bytes 1572868
  4.7 25.4 %copy-start.3 = (f32[1,256,512]{2,0,1:T(1,128)}, f32[1,256,512]{2,0,1:T(1,128)S(1)}, u32[]{:S(2)}) copy-start(f32[1,256,512]{2,0,1:T(1,128)S(1)} %stack.23) | copy-start | bytes 1572868
  4.7 9.2 %copy-start.18 = (s32[512,1]{0,1:T(1,128)S(1)}, s32[512,1]{0,1:T(1,128)}, u32[]{:S(2)}) copy-start(s32[512,1]{0,1:T(1,128)} %param.20) | copy-start | bytes 6148
  4.7 10.8 %copy-start.23 = (s32[512]{0:T(512)S(1)}, s32[512]{0:T(512)}, u32[]{:S(2)}) copy-start(s32[512]{0:T(512)} %param.21) | copy-start | bytes 6148
  6.7 1.4 copy-start.5
  8.1 21.9 %collective-permute-start = (f32[4,1,512]{2,0,1:T(4,128)S(1)}, f32[4,1,512]{2,0,1:T(4,128)S(1)}, u32[]{:S(2)}, u32[]{:S(2)}) collective-permute-start(f32[4,1,512]{2,0,1:T(4,128)S(1)} %get-tuple-element.17), channel_id=1, source_target_pairs={{8,0},{16,8},{24,16},{9,1},{17,9},{25,17},{10,2},{18,10},{26,18},{... | collective-permute-start | bytes 24584 | tf_op jit(solution)/shard_map/ppermute | solution.py:15
  9.4 20.7 %collective-permute-start.1 = (f32[4,1,512]{2,0,1:T(4,128)S(1)}, f32[4,1,512]{2,0,1:T(4,128)S(1)}, u32[]{:S(2)}, u32[]{:S(2)}) collective-permute-start(f32[4,1,512]{2,0,1:T(4,128)S(1)} %get-tuple-element.16), channel_id=1, source_target_pairs={{0,8},{8,16},{16,24},{1,9},{9,17},{17,25},{2,10},{10,18},{18,26},{... | collective-permute-start | bytes 24584 | tf_op jit(solution)/shard_map/ppermute | solution.py:12
  18.7 109.1 %all-to-all-start = ((f32[32,1,32]{2,1,0:T(1,128)}), f32[32,1,32]{2,1,0:T(1,128)S(1)}, u32[]{:S(2)}, u32[]{:S(2)}) async-start(f32[32,1,32]{2,1,0:T(1,128)} %all_to_all.12), calls=%async_computation | async-start | bytes 32768 | tf_op jit(solution)/shard_map/all_to_all | solution.py:87
  25.7 4.3 %copy-start.24 = (s32[512]{0:T(512)S(1)}, s32[512]{0:T(512)}, u32[]{:S(2)}) copy-start(s32[512]{0:T(512)} %param.19) | copy-start | bytes 6148
  32.1 1.4 copy-start
  34.9 11.9 %collective-permute-start.3 = (f32[4,258,1]{1,0,2:T(4,128)S(1)}, f32[4,258,1]{1,0,2:T(4,128)S(1)}, u32[]{:S(2)}, u32[]{:S(2)}) collective-permute-start(f32[4,258,1]{1,0,2:T(4,128)S(1)} %copy.61), channel_id=1, source_target_pairs={{0,1},{1,2},{2,3},{3,4},{4,5},{5,6},{6,7},{8,9},{9,10},{10,11},{11... | collective-permute-start | bytes 12392 | tf_op jit(solution)/shard_map/ppermute | solution.py:12
  43.1 34.5 %collective-permute-start.2 = (f32[4,258,1]{1,0,2:T(4,128)S(1)}, f32[4,258,1]{1,0,2:T(4,128)S(1)}, u32[]{:S(2)}, u32[]{:S(2)}) collective-permute-start(f32[4,258,1]{1,0,2:T(4,128)S(1)} %copy.58), channel_id=1, source_target_pairs={{1,0},{2,1},{3,2},{4,3},{5,4},{6,5},{7,6},{9,8},{10,9},{11,10},{12... | collective-permute-start | bytes 12392 | tf_op jit(solution)/shard_map/ppermute | solution.py:15
  47.9 15.5 %copy-start.2 = (f32[1,256,512]{2,0,1:T(1,128)S(1)}, f32[1,256,512]{2,0,1:T(1,128)}, u32[]{:S(2)}) copy-start(f32[1,256,512]{2,0,1:T(1,128)} %copy-done.1) | copy-start | bytes 1572868
  47.9 15.5 %copy-start.4 = (f32[1,256,512]{2,0,1:T(1,128)S(1)}, f32[1,256,512]{2,0,1:T(1,128)}, u32[]{:S(2)}) copy-start(f32[1,256,512]{2,0,1:T(1,128)} %copy-done.3) | copy-start | bytes 1572868
  47.9 15.5 %copy-start.7 = (f32[4,258,1]{2,0,1:T(4,128)S(1)}, f32[4,258,1]{2,0,1:T(4,128)}, u32[]{:S(2)}) copy-start(f32[4,258,1]{2,0,1:T(4,128)} %copy.62) | copy-start | bytes 12388
  77.9 5.4 %copy-start.6 = (f32[4,258,1]{2,1,0:T(8,128)}, f32[4,258,1]{2,1,0:T(8,128)S(1)}, u32[]{:S(2)}) copy-start(f32[4,258,1]{2,1,0:T(8,128)S(1)} %copy.60) | copy-start | bytes 12388
  83.2 2.8 %copy-start.8 = (s32[256,512]{1,0:T(8,128)S(1)}, s32[256,512]{1,0:T(8,128)}, u32[]{:S(2)}) copy-start(s32[256,512]{1,0:T(8,128)} %param.18) | copy-start | bytes 1572868
  90.8 2.2 %copy-start.11 = (f32[512,128]{1,0:T(8,128)S(1)}, f32[512,128]{1,0:T(8,128)}, u32[]{:S(2)}) copy-start(f32[512,128]{1,0:T(8,128)} %gather_fusion.1) | copy-start | bytes 786436
  90.8 2.2 %copy-start.22 = (f32[512]{0:T(512)S(1)}, f32[512]{0:T(512)}, u32[]{:S(2)}) copy-start(f32[512]{0:T(512)} %param.22) | copy-start | bytes 6148
  127.9 44.2 %all-to-all-start.1 = ((f32[32,32,3,128]{3,1,2,0:T(8,128)}), f32[32,32,3,128]{3,1,2,0:T(8,128)S(1)}, u32[]{:S(2)}, u32[]{:S(2)}) async-start(f32[32,32,3,128]{3,1,2,0:T(8,128)} %copy.68), calls=%async_computation.1 | async-start | bytes 3145728 | tf_op jit(solution)/shard_map/all_to_all | solution.py:80
  135.1 38.9 %copy-start.19 = (f32[16,128]{1,0:T(8,128)S(1)}, f32[16,128]{1,0:T(8,128)}, u32[]{:S(2)}) copy-start(f32[16,128]{1,0:T(8,128)} %param.25) | copy-start | bytes 24580
  135.1 38.9 %copy-start.20 = (f32[16,128]{1,0:T(8,128)S(1)}, f32[16,128]{1,0:T(8,128)}, u32[]{:S(2)}) copy-start(f32[16,128]{1,0:T(8,128)} %param.23) | copy-start | bytes 24580
  135.1 38.9 %copy-start.21 = (f32[16,128]{1,0:T(8,128)S(1)}, f32[16,128]{1,0:T(8,128)}, u32[]{:S(2)}) copy-start(f32[16,128]{1,0:T(8,128)} %param.24) | copy-start | bytes 24580
  174.0 5.1 %copy-start.15 = (f32[256,512]{1,0:T(8,128)S(1)}, f32[256,512]{1,0:T(8,128)}, u32[]{:S(2)}) copy-start(f32[256,512]{1,0:T(8,128)} %get-tuple-element.7) | copy-start | bytes 1572868
  174.4 4.8 %copy-start.16 = (f32[16,128]{1,0:T(8,128)}, f32[16,128]{1,0:T(8,128)S(1)}, u32[]{:S(2)}) copy-start(f32[16,128]{1,0:T(8,128)S(1)} %get-tuple-element.34) | copy-start | bytes 24580
  174.4 4.8 %copy-start.17 = (f32[16,128]{1,0:T(8,128)}, f32[16,128]{1,0:T(8,128)S(1)}, u32[]{:S(2)}) copy-start(f32[16,128]{1,0:T(8,128)S(1)} %get-tuple-element.35) | copy-start | bytes 24580
  176.1 30.2 %all-to-all-start.2 = ((f32[32,32,256]{2,1,0:T(8,128)}), f32[32,32,256]{2,1,0:T(8,128)S(1)}, u32[]{:S(2)}, u32[]{:S(2)}) async-start(f32[32,32,256]{2,1,0:T(8,128)} %bitcast.26), calls=%async_computation.2 | async-start | bytes 2097152 | tf_op jit(solution)/shard_map/all_to_all | solution.py:112
  206.3 1.7 copy-start.25
where the time goes:
time: 215 us; the launch traced here: 211 us
  local copies, waits for them, and re-layouts  67 us (31%)
  waiting for transfers between devices  64 us (30%)
  other arithmetic  47.8 us (22%)
  starting transfers between devices  27.6 us (13%)
  matrix products  3.33 us (2%)
    all_to_all x1, waiting for transfers between devices, body(): lax.all_to_all(outgoing.reshape(devices, slot_cap, 3, 128), ('row', 'col'...  37 us
    scatter x1, local copies, waits for them, and re-layouts, body(): jnp.zeros((devices * slot_cap, 3, 128), jnp.float32).at[slot_of]  31.4 us
    all_to_all x1, waiting for transfers between devices, body(): lax.all_to_all(reply.reshape(devices, slot_cap, 256), ('row', 'col'), spl...  27 us
    concatenate x2, other arithmetic, padded_2(): block = jnp.concatenate([low, block, high], axis=dim)  16.3 us
    slice x1, other arithmetic, body(): coeff = 0.5 * (conduct + beside[2]) * opened * beside[3]  15.4 us
    ppermute x2, starting transfers between devices, padded_2(): lax.ppermute(lax.slice_in_dim(block, block.shape[dim] - width, None, axis...  8.12 us
    unnamed x53, local copies, waits for them, and re-layouts  7.9 us
    all_to_all x1, starting transfers between devices, body(): lax.all_to_all(reach_tags.reshape(devices, slot_cap), ('row', 'col'), spl...  7.02 us
  transfers between devices with their start and end apart: 7, of which 2 were waited for; matrix products, arithmetic and copies ran while one was open for 47% of the time, Pallas kernels for 0%

commit v1 on v0

v1 whole, which is shorter than its diff:
```python
import functools

import jax
import jax.numpy as jnp
from jax import lax
from jax.experimental import pallas as pl
from jax.experimental.pallas import tpu as pltpu
from jax.sharding import PartitionSpec as P

MESH = pl.DeviceIdType.MESH
F32 = jnp.float32
BF16 = jnp.bfloat16
SEC = 128
BASE = 8
CHUNK = 16


def split(x):
    hi = x.astype(BF16)
    return hi, (x - hi.astype(F32)).astype(BF16)


def dot_nt(a, b):
    return lax.dot_general(a, b, (((1,), (1,)), ((), ())), preferred_element_type=F32)


def dot_nn(a, b):
    return jnp.dot(a, b, preferred_element_type=F32)


def smooth(v):
    lane = lax.broadcasted_iota(jnp.int32, v.shape, 1)
    left = jnp.where(lane == 0, v, pltpu.roll(v, 1, 1))
    right = jnp.where(lane == SEC - 1, v, pltpu.roll(v, SEC - 1, 1))
    return v + 0.25 * (left - 2.0 * v + right)


def kernel(
    n_row,
    n_col,
    depth_h,
    bed_h,
    mass_h,
    conduct_h,
    settle_h,
    wet_h,
    block_ref,
    reach_ref,
    coef_ref,
    phase_ref,
    conc_ref,
    area_ref,
    depth_out,
    mass_out,
    phase_out,
    conc_out,
    depth_v,
    bed_v,
    cond_v,
    settle_v,
    wet_v,
    s_pad,
    m_pad,
    c_pad,
    o_pad,
    d1,
    m1,
    s1,
    dcat,
    hot_l,
    hot_b,
    mat_hi,
    mat_lo,
    mt_hi,
    mt_lo,
    csum,
    part,
    r_core,
    q_row,
    r_row,
    s_z,
    r_z,
    table,
    row_send,
    row_recv,
    col_send,
    col_recv,
    in_sem,
    out_sem,
    halo_s,
    halo_r,
    core_s,
    core_r,
    row_s,
    row_r,
    z_s,
    z_r,
    gz_s,
    gz_r,
    gr_s,
    gr_r,
    gc_s,
    gc_r,
):
    rows, cols = depth_v.shape
    n_z = n_col // 2
    half = part.shape[2]
    nblk = cols // SEC
    r = lax.axis_index("row")
    c = lax.axis_index("col")
    k = lax.rem(c, 2)
    z = lax.div(c, 2)
    other = 1 - k

    loads = []
    data = (slice(BASE, BASE + rows), slice(0, cols))
    for i, (src, dst) in enumerate(
        (
            (wet_h, wet_v),
            (depth_h, depth_v),
            (bed_h, bed_v),
            (mass_h, m_pad.at[data]),
            (conduct_h, cond_v),
            (settle_h, settle_v),
        )
    ):
        loads.append(pltpu.make_async_copy(src, dst, in_sem.at[i]))
        loads[-1].start()

    core_dev = (r, 2 * z + other)
    row_devs = [(lax.rem(r + j, n_row), c) for j in range(1, n_row)]
    z_devs = [(r, 2 * lax.rem(z + j, n_z) + k) for j in range(1, n_z)]
    barrier = pltpu.get_barrier_semaphore()
    for dev in [core_dev] + row_devs + z_devs:
        pl.semaphore_signal(barrier, inc=1, device_id=dev, device_id_type=MESH)
    cross = c + 2 * k - 1
    has_cross = jnp.logical_and(cross >= 0, cross < n_col)

    @pl.when(has_cross)
    def _():
        pl.semaphore_signal(barrier, inc=1, device_id=(r, cross), device_id_type=MESH)

    block = block_ref[...]
    reach = reach_ref[...]
    coef = coef_ref[...]
    n_links = block.shape[1]
    chi, clo = split(coef)
    chi, clo = chi.astype(F32), clo.astype(F32)
    spot = lax.rem(block, nblk) * rows + lax.div(block, nblk)
    for b in range(nblk):
        ids = lax.broadcasted_iota(jnp.int32, (rows, n_links), 0) + b * rows
        hot_b[b * rows : (b + 1) * rows, :] = jnp.where(ids == spot, 1.0, 0.0).astype(BF16)
    for kk in range(2):
        ids = lax.broadcasted_iota(jnp.int32, (half, n_links), 0) + kk * half
        hit = ids == reach
        hot_l[0, kk * half : (kk + 1) * half, :] = jnp.where(hit, chi, 0.0).astype(BF16)
        hot_l[1, kk * half : (kk + 1) * half, :] = jnp.where(hit, clo, 0.0).astype(BF16)

    for kk in range(2):
        for b in range(nblk):
            here = hot_b[b * rows : (b + 1) * rows, :]
            m = dot_nt(hot_l[0, kk * half : (kk + 1) * half, :], here)
            m = m + dot_nt(hot_l[1, kk * half : (kk + 1) * half, :], here)
            hi, lo = split(m)
            mat_hi[kk, :, b * rows : (b + 1) * rows] = hi
            mat_lo[kk, :, b * rows : (b + 1) * rows] = lo

    for i in range(5):
        loads[i].wait()

    @pl.loop(0, rows // CHUNK)
    def _(i):
        at = pl.ds(pl.multiple_of(i * CHUNK, CHUNK), CHUNK)
        pad = pl.ds(pl.multiple_of(BASE + i * CHUNK, 8), CHUNK)
        o = wet_v[at, :].astype(F32)
        o_pad[pad, 0:cols] = o
        c_pad[pad, 0:cols] = (0.5 * cond_v[at, :]) * o
        s_pad[pad, 0:cols] = depth_v[at, :] + bed_v[at, :]
        for b in range(nblk):
            dst = pl.ds(pl.multiple_of(b * rows + i * CHUNK, CHUNK), CHUNK)
            dcat[0, dst, 0:SEC] = o[:, b * SEC : (b + 1) * SEC].astype(BF16)

    pads = (s_pad, m_pad, c_pad, o_pad)
    lane = lax.broadcasted_iota(jnp.int32, (rows, SEC), 1)
    packed = jnp.zeros((rows, SEC), F32)
    for j, ref in enumerate(pads):
        row_send[j : j + 1, :] = ref[BASE + rows - 1 : BASE + rows, 0:cols]
        row_send[4 + j : 5 + j, :] = ref[BASE : BASE + 1, 0:cols]
        packed = jnp.where(lane == j, ref[BASE : BASE + rows, cols - 1 : cols], packed)
        packed = jnp.where(lane == 4 + j, ref[BASE : BASE + rows, 0:1], packed)
    col_send[...] = packed.T[0:8, :]

    peers = 1 + len(row_devs) + len(z_devs)
    pl.semaphore_wait(barrier, jnp.where(has_cross, peers + 1, peers))

    def remote(src, dst, ssem, rsem, dev):
        return pltpu.make_async_remote_copy(
            src_ref=src, dst_ref=dst, send_sem=ssem, recv_sem=rsem, device_id=dev, device_id_type=MESH
        )

    halo = [
        (r + 1 < n_row, r > 0, remote(row_send, row_recv.at[0], halo_s.at[0], halo_r.at[0], (lax.rem(r + 1, n_row), c)), row_recv, 0),
        (r > 0, r + 1 < n_row, remote(row_send, row_recv.at[1], halo_s.at[1], halo_r.at[1], (lax.rem(r + n_row - 1, n_row), c)), row_recv, 1),
        (c + 1 < n_col, c > 0, remote(col_send, col_recv.at[0], halo_s.at[2], halo_r.at[2], (r, lax.rem(c + 1, n_col))), col_recv, 0),
        (c > 0, c + 1 < n_col, remote(col_send, col_recv.at[1], halo_s.at[3], halo_r.at[3], (r, lax.rem(c + n_col - 1, n_col))), col_recv, 1),
    ]
    for sends, gets, copy, buf, slot in halo:
        pl.when(sends)(copy.start)

        @pl.when(jnp.logical_not(gets))
        def _():
            buf[slot] = jnp.zeros(buf.shape[1:], F32)

    core_copy = [
        remote(part.at[p, other], r_core.at[p], core_s.at[p], core_r.at[p], core_dev) for p in range(3)
    ]
    row_copy = [
        [
            remote(q_row.at[p, dev[0]], r_row.at[p, j], row_s.at[p, j], row_r.at[p, j], dev)
            for j, dev in enumerate(row_devs)
        ]
        for p in range(3)
    ]
    z_copy = [
        [
            remote(s_z.at[p, lax.div(dev[1], 2)], r_z.at[p, j], z_s.at[p, j], z_r.at[p, j], dev)
            for j, dev in enumerate(z_devs)
        ]
        for p in range(3)
    ]

    def product(p, kk):
        if p == 0:
            d = dcat[0, :, 0:SEC]
            return dot_nn(mat_hi[kk], d) + dot_nn(mat_lo[kk], d)
        both = dot_nn(mat_hi[kk], dcat[p])
        return both[:, 0:SEC] + both[:, SEC:] + dot_nn(mat_lo[kk], dcat[p, :, 0:SEC])

    def stage_core(p):
        part[p, other] = product(p, other)
        core_copy[p].start()
        part[p, k] = product(p, k)

    def stage_row(p):
        core_copy[p].wait_recv()
        q_row[p] = (part[p, k] + r_core[p]).reshape(q_row.shape[1:])
        for copy in row_copy[p]:
            copy.start()

    def stage_z(p):
        total = q_row[p, r]
        for j, copy in enumerate(row_copy[p]):
            copy.wait_recv()
            total = total + r_row[p, j]
        s_z[p] = total.reshape(s_z.shape[1:])
        for copy in z_copy[p]:
            copy.start()

    def stage_sum(p):
        total = s_z[p, z]
        for j, copy in enumerate(z_copy[p]):
            copy.wait_recv()
            total = total + r_z[p, j]
        return total

    stage_core(0)

    for kk in range(2):
        for b in range(nblk):
            here = hot_b[b * rows : (b + 1) * rows, :]
            m = dot_nt(here, hot_l[0, kk * half : (kk + 1) * half, :])
            m = m + dot_nt(here, hot_l[1, kk * half : (kk + 1) * half, :])
            hi, lo = split(m)
            mt_hi[b * rows : (b + 1) * rows, kk * half : (kk + 1) * half] = hi
            mt_lo[b * rows : (b + 1) * rows, kk * half : (kk + 1) * half] = lo
            tot = jnp.broadcast_to(jnp.sum(m, axis=1, keepdims=True), (rows, SEC))
            at = slice(b * rows, (b + 1) * rows)
            csum[at, :] = tot if kk == 0 else csum[at, :] + tot
        if kk == 0:
            stage_row(0)

    loads[5].wait()
    for sends, gets, copy, buf, slot in halo:
        pl.when(gets)(copy.wait_recv)
    for j, ref in enumerate(pads):
        ref[BASE - 1 : BASE, 0:cols] = row_recv[0, j : j + 1, :]
        ref[BASE + rows : BASE + rows + 1, 0:cols] = row_recv[1, 4 + j : 5 + j, :]
    west = jnp.concatenate([col_recv[0], jnp.zeros((SEC - 8, rows), F32)], axis=0).T
    east = jnp.concatenate([col_recv[1], jnp.zeros((SEC - 8, rows), F32)], axis=0).T
    for j, ref in enumerate(pads):
        ref[BASE : BASE + rows, cols : cols + SEC] = jnp.where(
            lane == SEC - 1, west[:, j : j + 1], east[:, 4 + j : 5 + j]
        )

    wide = cols + SEC
    for y in range(0, rows, CHUNK):
        at = pl.ds(y, CHUNK)
        pad = pl.ds(y + BASE, CHUNK)
        up = pl.ds(y + BASE - 1, CHUNK)
        down = pl.ds(y + BASE + 1, CHUNK)
        s, m, co, o = (ref[pad, :] for ref in pads)

        def roll_left(v):
            return pltpu.roll(v, wide - 1, 1)

        o2 = roll_left(o)
        a = co * o2 + roll_left(co) * o
        fw = a * (roll_left(s) - s)
        fm = a * (roll_left(m) - m)
        gw = (fw - pltpu.roll(fw, 1, 1))[:, 0:cols]
        gm = (fm - pltpu.roll(fm, 1, 1))[:, 0:cols]
        s, m, co, o = (v[:, 0:cols] for v in (s, m, co, o))
        for side in (up, down):
            a = co * o_pad[side, 0:cols] + c_pad[side, 0:cols] * o
            gw = gw + a * (s_pad[side, 0:cols] - s)
            gm = gm + a * (m_pad[side, 0:cols] - m)
        d1[at, :] = depth_v[at, :] + gw
        surf = s + gw
        s1[at, :] = surf
        mm = (m + gm) * jnp.exp(-settle_v[at, :])
        m1[at, :] = mm
        for p, v in ((1, o * surf), (2, o * mm)):
            hi, lo = split(v)
            for b in range(nblk):
                dst = pl.ds(b * rows + y, CHUNK)
                dcat[p, dst, 0:SEC] = hi[:, b * SEC : (b + 1) * SEC]
                dcat[p, dst, SEC : 2 * SEC] = lo[:, b * SEC : (b + 1) * SEC]

    stage_core(1)
    stage_z(0)
    stage_core(2)
    stage_row(1)
    stage_row(2)
    area = area_ref[...]
    rcp = 1.0 / (area + stage_sum(0))
    stage_z(1)
    stage_z(2)

    gz = [
        [
            remote(table.at[t, k, r, z], table.at[t, k, r, z], gz_s.at[t, j], gz_r.at[t, j], dev)
            for j, dev in enumerate(z_devs)
        ]
        for t in range(2)
    ]
    gr = [
        [
            remote(table.at[t, k, r], table.at[t, k, r], gr_s.at[t, j], gr_r.at[t, j], dev)
            for j, dev in enumerate(row_devs)
        ]
        for t in range(2)
    ]
    gc = [
        [
            remote(
                table.at[t, k, lax.rem(r + n_row - j, n_row)],
                table.at[t, k, lax.rem(r + n_row - j, n_row)],
                gc_s.at[t, j],
                gc_r.at[t, j],
                core_dev,
            )
            for j in range(n_row)
        ]
        for t in range(2)
    ]

    for t, (chan, out) in enumerate(((phase_ref, phase_out), (conc_ref, conc_out))):
        new = smooth((area * chan[...] + stage_sum(t + 1)) * rcp)
        out[...] = new
        table[t, k, r, z] = new
        for copy in gz[t]:
            copy.start()
    for t in range(2):
        for copy in gz[t]:
            copy.wait_recv()
        for copy in gr[t]:
            copy.start()
        gc[t][0].start()
    for t in range(2):
        for j in range(1, n_row):
            gr[t][j - 1].wait_recv()
            gc[t][j].start()
    stores = []
    for t, (src, base, ref, out) in enumerate(((s1, d1, d1, depth_out), (m1, m1, m1, mass_out))):
        for copy in gc[t]:
            copy.wait_recv()
        hi, lo = split(table[t].reshape(2 * half, SEC))
        both = jnp.concatenate([hi, lo], axis=1)
        for b in range(nblk):
            at = slice(b * rows, (b + 1) * rows)
            x = slice(b * SEC, (b + 1) * SEC)
            g = dot_nn(mt_hi[at, :], both)
            g = g[:, 0:SEC] + g[:, SEC:] + dot_nn(mt_lo[at, :], hi)
            o = o_pad[BASE : BASE + rows, x]
            ref[:, x] = base[:, x] + 0.5 * o * (g - csum[at, :] * src[:, x])
        stores.append(pltpu.make_async_copy(ref, out, out_sem.at[t]))
        stores[-1].start()

    for copy in stores:
        copy.wait()
    for sends, gets, copy, buf, slot in halo:
        pl.when(sends)(copy.wait_send)
    for p in range(3):
        core_copy[p].wait_send()
        for copy in row_copy[p] + z_copy[p]:
            copy.wait_send()
    for t in range(2):
        for copy in gz[t] + gr[t] + gc[t]:
            copy.wait_send()


def body(n_row, n_col, *args):
    depth, bed, mass, conduct, settle, wet, block, owner, reach, coef, phase, conc, area = args
    rows, cols = depth.shape
    n_links = block.shape[0]
    reach_dev = phase.shape[0]
    n_z = n_col // 2
    cells = rows * cols // SEC
    total = n_row * n_col * reach_dev
    half = total // 2
    target = owner[:, 0]
    line = target % n_col
    place = (((line % 2) * n_row + target // n_col) * n_z + line // 2) * reach_dev + reach
    row = (1, n_links)
    vm = pl.BlockSpec(memory_space=pltpu.VMEM)
    hbm = pl.BlockSpec(memory_space=pl.ANY)
    dma = pltpu.SemaphoreType.DMA
    tile = pltpu.VMEM((rows, cols), F32)
    pad = pltpu.VMEM((rows + 2 * BASE, cols + SEC), F32)
    like = lambda a: jax.ShapeDtypeStruct(a.shape, F32)
    return pl.pallas_call(
        functools.partial(kernel, n_row, n_col),
        out_shape=(like(depth), like(mass), like(phase), like(conc)),
        in_specs=[hbm] * 6 + [vm] * 6,
        out_specs=(hbm, hbm, vm, vm),
        scratch_shapes=[
            tile,
            tile,
            tile,
            tile,
            pltpu.VMEM((rows, cols), jnp.int32),
            pad,
            pad,
            pad,
            pad,
            tile,
            tile,
            tile,
            pltpu.VMEM((3, cells, 2 * SEC), BF16),
            pltpu.VMEM((2, total, n_links), BF16),
            pltpu.VMEM((cells, n_links), BF16),
            pltpu.VMEM((2, half, cells), BF16),
            pltpu.VMEM((2, half, cells), BF16),
            pltpu.VMEM((cells, total), BF16),
            pltpu.VMEM((cells, total), BF16),
            pltpu.VMEM((cells, SEC), F32),
            pltpu.VMEM((3, 2, half, SEC), F32),
            pltpu.VMEM((3, half, SEC), F32),
            pltpu.VMEM((3, n_row, half // n_row, SEC), F32),
            pltpu.VMEM((3, n_row - 1, half // n_row, SEC), F32),
            pltpu.VMEM((3, n_z, reach_dev, SEC), F32),
            pltpu.VMEM((3, n_z - 1, reach_dev, SEC), F32),
            pltpu.VMEM((2, 2, n_row, n_z, reach_dev, SEC), F32),
            pltpu.VMEM((8, cols), F32),
            pltpu.VMEM((2, 8, cols), F32),
            pltpu.VMEM((8, rows), F32),
            pltpu.VMEM((2, 8, rows), F32),
            dma((6,)),
            dma((2,)),
            dma((4,)),
            dma((4,)),
            dma((3,)),
            dma((3,)),
            dma((3, n_row - 1)),
            dma((3, n_row - 1)),
            dma((3, n_z - 1)),
            dma((3, n_z - 1)),
            dma((2, n_z - 1)),
            dma((2, n_z - 1)),
            dma((2, n_row - 1)),
            dma((2, n_row - 1)),
            dma((2, n_row)),
            dma((2, n_row)),
        ],
        compiler_params=pltpu.CompilerParams(
            collective_id=0, has_side_effects=True, vmem_limit_bytes=56 * 2**20
        ),
    )(
        depth,
        bed,
        mass,
        conduct,
        settle,
        wet,
        block.reshape(row),
        place.reshape(row),
        coef.reshape(row),
        phase,
        conc,
        area,
    )


def solution(mesh):
    both = P(("row", "col"))
    return jax.shard_map(
        functools.partial(body, mesh.shape["row"], mesh.shape["col"]),
        mesh=mesh,
        in_specs=(P("row", "col"),) * 6 + (both,) * 7,
        out_specs=(P("row", "col"), P("row", "col"), both, both),
        check_vma=False,
    )
```

time: 215 us -> 39.2 us (0.18); the launches traced: 211 us -> 38.8 us
  waiting for transfers between devices: 64 us -> 0 us
  local copies, waits for them, and re-layouts: 67 us -> 4.71 us
  other arithmetic: 47.8 us -> 0.6 us
  Pallas kernels: 0 us -> 32.9 us
  starting transfers between devices: 27.6 us -> 0 us
  matrix products: 3.33 us -> 0 us
    all_to_all x3 -> x0, waiting for transfers between devices: 64 us -> none  [the longest x1 37 us: body(): lax.all_to_all(outgoing.reshape(devices, slot_cap, 3, 128), ('row', 'col'...]
    scatter x2 -> x0, local copies, waits for them, and re-layouts: 33.8 us -> none  [the longest x1 31.4 us: body(): jnp.zeros((devices * slot_cap, 3, 128), jnp.float32).at[slot_of]]
    pallas_call x0 -> x1, Pallas kernels: none -> 32.9 us  [body(): pl.pallas_call(functools.partial(kernel, n_row, n_col), out_shape=(like(d...]
    concatenate x2 -> x0, other arithmetic: 16.3 us -> none  [padded_2(): block = jnp.concatenate([low, block, high], axis=dim)]
    all_to_all x3 -> x0, starting transfers between devices: 16.1 us -> none  [the longest x1 7.02 us: body(): lax.all_to_all(reach_tags.reshape(devices, slot_cap), ('row', 'col'), spl...]
    slice x1 -> x0, other arithmetic: 15.4 us -> none  [body(): coeff = 0.5 * (conduct + beside[2]) * opened * beside[3]]
    ppermute x4 -> x0, starting transfers between devices: 11.5 us -> none  [the longest x2 8.12 us: padded_2(): lax.ppermute(lax.slice_in_dim(block, block.shape[dim] - width, None, axis...]
    reshape x7 -> x0, local copies, waits for them, and re-layouts: 5.46 us -> none  [the longest x1 1.39 us: body(): outgoing.reshape(devices, slot_cap, 3, 128)]
  transfers between devices with their start and end apart: 7 -> 0, of which waited for: 2 -> 0; matrix products, arithmetic and copies ran while one was open for 47% -> 0% of each run, Pallas kernels for 0% -> 0%
where the time goes in v1:
time: 39.2 us; the launch traced here: 38.8 us
  Pallas kernels  32.9 us (84%)
  local copies, waits for them, and re-layouts  4.71 us (12%)
  between operations  0.67 us (2%)
  other arithmetic  0.6 us (2%)
    pallas_call x1, Pallas kernels, body(): pl.pallas_call(functools.partial(kernel, n_row, n_col), out_shape=(like(d...  32.9 us
    unnamed x14, local copies, waits for them, and re-layouts  4.71 us

profile of v1, /device:TPU:1, one launch (start us, length us, event | category | flops | bytes accessed | tf_op | source)
XLA Modules:
  0.0 38.8 jit_solution(10249897913460200002)
XLA Ops:
  0.6 0.0 copy-start.4
  0.6 0.0 copy-start.3
  0.7 0.7 %copy-done.4 = s32[512,1]{0,1:T(1,128)S(1)} copy-done((s32[512,1]{0,1:T(1,128)S(1)}, s32[512,1]{0,1:T(1,128)}, u32[]{:S(2)}) %copy-start.4) | copy-done | bytes 2072
  1.3 0.0 copy-done.3
  1.3 0.6 %fusion.5 = s32[512]{0:T(512)} fusion(s32[512]{0:T(512)S(1)} %copy-done.3, s32[512]{0:T(512)S(1)} %bitcast.5), kind=kLoop, calls=%fused_computation.15 | loop fusion | flops 22528 | bytes 6144 | tf_op jit(solution)/shard_map/add | solution.py:423
  1.9 32.9 %shard_map.156 = (f32[256,512]{1,0:T(8,128)}, f32[256,512]{1,0:T(8,128)}, f32[16,128]{1,0:T(8,128)}, f32[16,128]{1,0:T(8,128)}) custom-call(f32[256,512]{1,0:T(8,128)} %depth_h.1, f32[256,512]{1,0:T(8,128)} %bed_h.1, f32[256,512]{1,0:T(8,128)} %mass_h.1, f32[256,512]{1,0:T(8,128)} %conduct_h.1, f32[256,512]{1,0:T(8,128)} %settle_h.1, s32[256,512]{1,0:T(8,128)} %wet_h.1, ...), custom_call_target="tpu_custom_call" | custom-call | tf_op jit(solution)/shard_map/pallas_call | solution.py:431
  34.8 0.0 copy-start
  34.8 1.9 %copy.21 = f32[256,512]{1,0:T(8,128)} copy(f32[256,512]{1,0:T(8,128)} %get-tuple-element.8) | data formatting | bytes 1048576
  36.7 0.0 copy-done
  36.7 0.0 copy-start.2
  36.7 0.8 %copy.22 = f32[256,512]{1,0:T(8,128)} copy(f32[256,512]{1,0:T(8,128)S(1)} %copy-done) | data formatting | bytes 1048576
  37.5 0.0 copy-done.2
  37.5 0.0 copy-start.1
  37.5 0.6 %copy.23 = f32[16,128]{1,0:T(8,128)} copy(f32[16,128]{1,0:T(8,128)S(1)} %copy-done.2) | data formatting | bytes 16384
  38.1 0.1 copy-done.1
  38.2 0.6 %copy.24 = f32[16,128]{1,0:T(8,128)} copy(f32[16,128]{1,0:T(8,128)S(1)} %copy-done.1) | data formatting | bytes 16384
Async XLA Ops:
  0.6 0.7 %copy-start.4 = (s32[512,1]{0,1:T(1,128)S(1)}, s32[512,1]{0,1:T(1,128)}, u32[]{:S(2)}) copy-start(s32[512,1]{0,1:T(1,128)} %param.20) | copy-start | bytes 6148
  0.6 0.7 %copy-start.3 = (s32[512]{0:T(512)S(1)}, s32[512]{0:T(512)}, u32[]{:S(2)}) copy-start(s32[512]{0:T(512)} %param.21) | copy-start | bytes 6148
  34.8 1.9 %copy-start = (f32[256,512]{1,0:T(8,128)S(1)}, f32[256,512]{1,0:T(8,128)}, u32[]{:S(2)}) copy-start(f32[256,512]{1,0:T(8,128)} %get-tuple-element.9) | copy-start | bytes 1572868
  36.7 0.8 %copy-start.2 = (f32[16,128]{1,0:T(8,128)S(1)}, f32[16,128]{1,0:T(8,128)}, u32[]{:S(2)}) copy-start(f32[16,128]{1,0:T(8,128)} %get-tuple-element.10) | copy-start | bytes 24580
  37.5 0.7 %copy-start.1 = (f32[16,128]{1,0:T(8,128)S(1)}, f32[16,128]{1,0:T(8,128)}, u32[]{:S(2)}) copy-start(f32[16,128]{1,0:T(8,128)} %get-tuple-element.11) | copy-start | bytes 24580

commit v2 on v1

--- a/solution.py
+++ b/solution.py
@@ -13,6 +13,7 @@
 SEC = 128
 BASE = 8
 CHUNK = 16
+PIECES = 4
 
 
 def split(x):
@@ -45,6 +46,7 @@
     settle_h,
     wet_h,
     block_ref,
+    owner_ref,
     reach_ref,
     coef_ref,
     phase_ref,
@@ -141,7 +143,10 @@
         pl.semaphore_signal(barrier, inc=1, device_id=(r, cross), device_id_type=MESH)
 
     block = block_ref[...]
-    reach = reach_ref[...]
+    target = owner_ref[...]
+    line = lax.rem(target, n_col)
+    reach = (lax.rem(line, 2) * n_row + lax.div(target, n_col)) * n_z + lax.div(line, 2)
+    reach = reach * phase_ref.shape[0] + reach_ref[...]
     coef = coef_ref[...]
     n_links = block.shape[1]
     chi, clo = split(coef)
@@ -409,6 +414,21 @@
             copy.wait_send()
 
 
+def hand_on(*refs):
+    sems = refs[8]
+    copies = []
+    for i in range(4):
+        rows = refs[i].shape[0]
+        step = rows // PIECES if rows >= 8 * PIECES else rows
+        for j, y in enumerate(range(0, rows, step)):
+            at = pl.ds(y, step)
+            copies.append(pltpu.make_async_copy(refs[i].at[at], refs[4 + i].at[at], sems.at[i, j]))
+    for copy in copies:
+        copy.start()
+    for copy in copies:
+        copy.wait()
+
+
 def body(n_row, n_col, *args):
     depth, bed, mass, conduct, settle, wet, block, owner, reach, coef, phase, conc, area = args
     rows, cols = depth.shape
@@ -418,9 +438,6 @@
     cells = rows * cols // SEC
     total = n_row * n_col * reach_dev
     half = total // 2
-    target = owner[:, 0]
-    line = target % n_col
-    place = (((line % 2) * n_row + target // n_col) * n_z + line // 2) * reach_dev + reach
     row = (1, n_links)
     vm = pl.BlockSpec(memory_space=pltpu.VMEM)
     hbm = pl.BlockSpec(memory_space=pl.ANY)
@@ -428,10 +445,10 @@
     tile = pltpu.VMEM((rows, cols), F32)
     pad = pltpu.VMEM((rows + 2 * BASE, cols + SEC), F32)
     like = lambda a: jax.ShapeDtypeStruct(a.shape, F32)
-    return pl.pallas_call(
+    made = pl.pallas_call(
         functools.partial(kernel, n_row, n_col),
         out_shape=(like(depth), like(mass), like(phase), like(conc)),
-        in_specs=[hbm] * 6 + [vm] * 6,
+        in_specs=[hbm] * 6 + [vm] * 7,
         out_specs=(hbm, hbm, vm, vm),
         scratch_shapes=[
             tile,
@@ -493,12 +510,21 @@
         settle,
         wet,
         block.reshape(row),
-        place.reshape(row),
+        owner.reshape(row),
+        reach.reshape(row),
         coef.reshape(row),
         phase,
         conc,
         area,
     )
+    return pl.pallas_call(
+        hand_on,
+        out_shape=tuple(like(a) for a in made),
+        in_specs=[hbm] * 4,
+        out_specs=(hbm,) * 4,
+        scratch_shapes=[dma((4, PIECES))],
+        compiler_params=pltpu.CompilerParams(vmem_limit_bytes=60 * 2**20),
+    )(*made)
 
 
 def solution(mesh):

time: 39.2 us -> 67.3 us (1.72)
  Pallas kernels: 32.9 us -> 66.4 us
  local copies, waits for them, and re-layouts: 4.71 us -> 0 us
    pallas_call x0 -> x1, Pallas kernels: none -> 33.5 us  [body(): pl.pallas_call(hand_on, out_shape=tuple((like(a) for a in made)), in_spec...]
    unnamed x14 -> x0, local copies, waits for them, and re-layouts: 4.71 us -> none
where the time goes in v2:
time: 67.3 us; the launch traced here: 67 us
  Pallas kernels  66.4 us (99%)
    pallas_call x1, Pallas kernels, body(): pl.pallas_call(hand_on, out_shape=tuple((like(a) for a in made)), in_spec...  33.5 us
    pallas_call x1, Pallas kernels, body(): pl.pallas_call(functools.partial(kernel, n_row, n_col), out_shape=(like(d...  32.9 us

profile of v2, /device:TPU:1, one launch (start us, length us, event | category | flops | bytes accessed | tf_op | source)
XLA Modules:
  0.0 67.0 jit_solution(11519073348233176569)
XLA Ops:
  0.6 32.9 %shard_map.156 = (f32[256,512]{1,0:T(8,128)}, f32[256,512]{1,0:T(8,128)}, f32[16,128]{1,0:T(8,128)}, f32[16,128]{1,0:T(8,128)}) custom-call(f32[256,512]{1,0:T(8,128)} %depth_h.1, f32[256,512]{1,0:T(8,128)} %bed_h.1, f32[256,512]{1,0:T(8,128)} %mass_h.1, f32[256,512]{1,0:T(8,128)} %conduct_h.1, f32[256,512]{1,0:T(8,128)} %settle_h.1, s32[256,512]{1,0:T(8,128)} %wet_h.1, ...), custom_call_target="tpu_custom_call" | custom-call | tf_op jit(solution)/shard_map/pallas_call | solution.py:448
  33.5 33.5 %shard_map.157 = (f32[256,512]{1,0:T(8,128)}, f32[256,512]{1,0:T(8,128)}, f32[16,128]{1,0:T(8,128)}, f32[16,128]{1,0:T(8,128)}) custom-call(f32[256,512]{1,0:T(8,128)} %get-tuple-element.8.refs_0_, f32[256,512]{1,0:T(8,128)} %get-tuple-element.9.refs_1_, f32[16,128]{1,0:T(8,128)} %get-tuple-element.10.refs_2_, f32[16,128]{1,0:T(8,128)} %get-tuple-element.11.refs_3_), custom_call_target="tpu_custom_call" | custom-call | tf_op jit(solution)/shard_map/pallas_call | solution.py:520
